TPU v7x, 32 devices: a whole 2x2x4 slice. The times are simulated.
32 devices in a mesh: groups: 1, wide: 32 (over z, y, x, core).
Axes of the slice: x: 2, y: 2, z: 4, core: 2. Of those that a mesh axis runs over, the one named last changes fastest.
Arguments:
- queries: bfloat16 [256, 1152], P('groups'), may hold values from -4 to 4
- patch_keys: bfloat16 [4096, 1152], P(('groups', 'wide')), may hold values from -173 to 173
- patch_values: bfloat16 [4096, 2560], P(('groups', 'wide')), may hold values from -6 to 6
- norm_gain: float32 [2560], replicated, may hold values from 0.1 to 1.9
- route_experts: int32 [512, 6], P(('groups', 'wide')), may hold values from 0 to 15, all different within a row; in each aligned block of 16 rows (0 to 15, 16 to 31, ...) at most 16 rows name the same one
- route_weights: int32 [512, 6], P(('groups', 'wide')), may hold values from 1 to 16
- w_gate: bfloat16 [16384, 2560], P('wide'), may hold values from -0.125 to 0.125
- w_up: bfloat16 [16384, 2560], P('wide'), may hold values from -0.125 to 0.125
- w_down: bfloat16 [16384, 2560], P('wide'), may hold values from -0.1875 to 0.1875
Outputs:
- mixed_rows: bfloat16 [512, 2560], P(('groups', 'wide'))
Inputs may be any that keep to these rules, and one draw needn't show every extreme that they name: `route_experts`: each row names 6 different experts. In each aligned block of 16 rows (the rows of one device) no expert is named by more than 16 rows, a bound that some block reaches.
All inputs are finite; a program needn't handle non-finite values.
Results may differ from a plain program's by a relative error of at most 0.02.
Values may be sent and summed in bfloat16 or wider, within the bound.
A program may use at most 128 MiB of HBM per device.

v0:
```python
import jax
import jax.numpy as jnp
from jax import lax
from jax.sharding import PartitionSpec as P

HEADS = 16


def partner(value, axis, stride):
    mask = 2**stride
    pairs = [(source, source ^ mask) for source in range(lax.axis_size(axis))]
    return lax.ppermute(value, axis, pairs)


def merge_partials(first_part, second_part, head_count):
    sum_first, peak_first, total_first = first_part
    sum_second, peak_second, total_second = second_part
    row_peak = jnp.maximum(peak_first, peak_second)
    factor_first = jnp.exp(peak_first - row_peak)
    factor_second = jnp.exp(peak_second - row_peak)
    row_total = total_first * factor_first + total_second * factor_second
    row_count = sum_first.shape[0]
    summed = sum_first.reshape(row_count, head_count, -1) * factor_first[:, :, None]
    summed = summed + sum_second.reshape(row_count, head_count, -1) * factor_second[:, :, None]
    return (summed.reshape(row_count, -1), row_peak, row_total)


def on_device(
    queries, patch_keys, patch_values, norm_gain, route_experts, route_weights, w_gate, w_up, w_down
):
    row_count = route_experts.shape[0]
    top_k = route_experts.shape[1]
    model_width = patch_values.shape[1]
    vision_width = patch_keys.shape[1]
    head_count = HEADS
    key_size = vision_width // head_count
    value_size = model_width // head_count
    group_size = queries.shape[0] // row_count
    levels = group_size.bit_length() - 1
    devices = lax.axis_size("wide")
    device_index = lax.axis_index("wide")
    score_scale = key_size ** (-0.5)
    scores = (
        jnp.einsum(
            "qhc,phc->qhp",
            queries.reshape(-1, head_count, key_size),
            patch_keys.reshape(-1, head_count, key_size),
            preferred_element_type=jnp.float32,
        )
        * score_scale
    )
    row_peak = jnp.max(scores, axis=2)
    raised = jnp.exp(scores - row_peak[:, :, None])
    row_total = jnp.sum(raised, axis=2)
    summed = jnp.einsum(
        "qhp,phc->qhc",
        raised.astype(jnp.bfloat16),
        patch_values.reshape(-1, head_count, value_size),
        preferred_element_type=jnp.float32,
    ).reshape(-1, model_width)
    for bit_number in reversed(range(levels)):
        half_rows = summed.shape[0] // 2
        upper_half = device_index // (1 << bit_number) % 2 == 1
        kept_part = (
            jnp.where(upper_half, summed[half_rows:], summed[:half_rows]),
            jnp.where(upper_half, row_peak[half_rows:], row_peak[:half_rows]),
            jnp.where(upper_half, row_total[half_rows:], row_total[:half_rows]),
        )
        sent_sum = jnp.where(upper_half, summed[:half_rows], summed[half_rows:])
        sent_peak = jnp.where(upper_half, row_peak[:half_rows], row_peak[half_rows:])
        sent_total = jnp.where(upper_half, row_total[:half_rows], row_total[half_rows:])
        partner_part = partner((sent_sum, sent_peak, sent_total), "wide", bit_number)
        summed, row_peak, row_total = merge_partials(kept_part, partner_part, head_count)
    attended = summed.reshape(row_count, head_count, value_size) / row_total[:, :, None]
    projected = attended.reshape(row_count, model_width).astype(jnp.bfloat16)
    residual = projected.astype(jnp.float32)
    normed = (
        residual
        * lax.rsqrt(jnp.mean(residual * residual, axis=1, keepdims=True) + 1e-06)
        * norm_gain
    ).astype(jnp.bfloat16)
    experts = devices // 2
    capacity = 32 * row_count // devices
    flat_routes = route_experts.reshape(-1)
    onehot = (flat_routes[:, None] == jnp.arange(experts, dtype=jnp.int32)[None, :]).astype(
        jnp.int32
    )
    earlier = jnp.cumsum(onehot, axis=0) - onehot
    slot_index = jnp.sum(earlier * onehot, axis=1)
    position = flat_routes * capacity + slot_index
    placing = jnp.any(
        position.reshape(row_count, top_k)[:, :, None]
        == jnp.arange(experts * capacity, dtype=jnp.int32)[None, None, :],
        axis=1,
    )
    buffer = lax.dot_general(
        placing.astype(jnp.bfloat16),
        normed,
        (((0,), (0,)), ((), ())),
        preferred_element_type=jnp.float32,
    ).astype(jnp.bfloat16)
    sent_rows = jnp.broadcast_to(
        buffer.reshape(experts, 1, capacity, model_width), (experts, 2, capacity, model_width)
    ).reshape(devices, capacity, model_width)
    received = lax.all_to_all(sent_rows, "wide", split_axis=0, concat_axis=0, tiled=True)
    sources, item_count, row_width = received.shape
    flat_rows = received.reshape(sources * item_count, row_width)
    gate_part = lax.dot_general(
        w_gate, flat_rows, (((1,), (1,)), ((), ())), preferred_element_type=jnp.float32
    )
    up_part = lax.dot_general(
        w_up, flat_rows, (((1,), (1,)), ((), ())), preferred_element_type=jnp.float32
    )
    hidden = (jax.nn.silu(gate_part) * up_part).astype(jnp.bfloat16)
    partial_value = lax.dot_general(
        hidden, w_down, (((0,), (0,)), ((), ())), preferred_element_type=jnp.float32
    )
    partial_value = partial_value.reshape(sources, item_count, row_width)
    returned = lax.all_to_all(
        partial_value.astype(jnp.bfloat16), "wide", split_axis=0, concat_axis=0, tiled=True
    ).astype(partial_value.dtype)
    outputs = (
        jnp.sum(returned.reshape(experts, 2, -1, model_width), axis=1)
        .astype(jnp.bfloat16)
        .reshape(-1, model_width)
    )
    picked = (
        jnp.take(outputs, position, axis=0)
        .reshape(row_count, top_k, model_width)
        .astype(jnp.float32)
    )
    scores_int = route_weights.astype(jnp.float32)
    gate_share = scores_int / jnp.sum(scores_int, axis=1, keepdims=True)
    mixed_rows = residual + jnp.sum(picked * gate_share[:, :, None], axis=1)
    return mixed_rows.astype(jnp.bfloat16)


def solution(mesh):
    return jax.shard_map(
        on_device,
        mesh=mesh,
        in_specs=(
            P("groups", None),
            P(("groups", "wide"), None),
            P(("groups", "wide"), None),
            P(),
            P(("groups", "wide"), None),
            P(("groups", "wide"), None),
            P("wide", None),
            P("wide", None),
            P("wide", None),
        ),
        out_specs=P(("groups", "wide"), None),
        check_vma=False,
    )
```

profile of v0, /device:TPU:0, one launch (start us, length us, event | category | flops | bytes accessed | tf_op | source)
XLA Modules:
  0.0 246.0 jit_solution(1788478821131541885)
XLA Ops:
  0.0 1.3 copy.40
  1.3 1.3 copy.41
  2.6 0.5 bitcast_reduce_fusion.1
  3.1 1.3 copy-done.5
  4.5 0.4 fusion.1
  4.9 3.1 %collective-permute-start.8 = (f32[128,16]{0,1:T(8,128)S(1)}, f32[128,16]{0,1:T(8,128)S(1)}, u32[]{:S(2)}, u32[]{:S(2)}) collective-permute-start(f32[128,16]{0,1:T(8,128)S(1)} %slice_select_fusion.7), channel_id=1, source_target_pairs={{0,8},{1,9},{2,10},{3,11},{4,12},{5,13},{6,14},{7,15},{8,0},{9,1},... | collective-permute-start | bytes 24584 | tf_op jit(solution)/shard_map/ppermute | solution.py:12
  8.0 0.1 collective-permute-start
  8.1 1.4 copy.42
  9.5 2.1 convolution_bitcast_fusion
  11.6 1.3 slice_select_fusion.3
  12.9 0.6 copy-done.4
  13.6 1.9 collective-permute-start.1
  15.5 0.1 copy.50
  15.6 0.1 reshape.148
  15.7 0.1 fusion.13
  15.8 0.1 reduce_window_sum.11
  15.9 0.2 select_reduce_fusion
  16.3 1.5 collective-permute-start.2
  17.9 0.5 collective-permute-start.9
  18.5 1.5 collective-permute-done.2
  20.0 1.6 collective-permute-done.9
  21.7 22.5 %collective-permute-done.1 = f32[128,2560]{0,1:T(8,128)} collective-permute-done((f32[128,2560]{0,1:T(8,128)}, f32[128,2560]{0,1:T(8,128)}, u32[]{:S(2)}, u32[]{:S(2)}) %collective-permute-start.1) | collective-permute-done | bytes 1310752 | tf_op jit(solution)/shard_map/ppermute | solution.py:12
  44.1 2.5 %multiply_add_fusion.2 = f32[128,16,160]{0,2,1:T(8,128)S(1)} fusion(f32[128,16,160]{0,2,1:T(8,128)} %bitcast.6, f32[256,16,160]{0,2,1:T(8,128)} %copy-done.4, f32[128,16]{0,1:T(8,128)S(1)} %get-tuple-element.22, f32[128,16]{0,1:T(8,128)S(1)} %get-tuple-element.21, pred[]{:T(512)S(6)} %eq.46), kind=kLoop, calls=%fused_computation.19 | loop fusion | flops 1310720 | bytes 5259265 | tf_op jit(solution)/shard_map/add | solution.py:24
  46.6 1.5 slice_select_fusion.2
  48.1 1.7 copy.44
  49.8 1.7 collective-permute-start.3
  51.6 1.5 collective-permute-start.4
  53.1 0.5 collective-permute-start.10
  53.8 1.4 collective-permute-done.4
  55.2 1.6 collective-permute-done.10
  56.8 0.1 multiply_add_fusion.4
  56.9 8.4 %collective-permute-done.3 = f32[64,2560]{1,0:T(8,128)} collective-permute-done((f32[64,2560]{1,0:T(8,128)S(1)}, f32[64,2560]{1,0:T(8,128)}, u32[]{:S(2)}, u32[]{:S(2)}) %collective-permute-start.3) | collective-permute-done | bytes 655392 | tf_op jit(solution)/shard_map/ppermute | solution.py:12
  65.3 2.6 %copy.45 = f32[64,2560]{0,1:T(8,128)} copy(f32[64,2560]{1,0:T(8,128)} %collective-permute-done.3) | data formatting | bytes 1310720 | tf_op jit(solution)/shard_map/ppermute | solution.py:12
  67.8 2.6 %multiply_add_fusion.1 = f32[64,16,160]{0,2,1:T(8,128)S(1)} fusion(f32[64,16,160]{0,2,1:T(8,128)} %bitcast.64, f32[128,16,160]{0,2,1:T(8,128)} %copy-done.1, f32[64,16]{0,1:T(8,128)S(1)} %get-tuple-element.18, f32[64,16]{0,1:T(8,128)S(1)} %get-tuple-element.17, pred[]{:T(512)S(6)} %eq.45), kind=kLoop, calls=%fused_computation.18 | loop fusion | flops 655360 | bytes 2629633 | tf_op jit(solution)/shard_map/add | solution.py:24
  70.4 1.5 slice_select_fusion.1
  71.9 1.7 copy.46
  73.6 1.3 collective-permute-start.5
  75.1 0.5 collective-permute-start.11
  75.6 5.4 %collective-permute-done.5 = f32[32,2560]{1,0:T(8,128)S(1)} collective-permute-done((f32[32,2560]{1,0:T(8,128)S(1)}, f32[32,2560]{1,0:T(8,128)S(1)}, u32[]{:S(2)}, u32[]{:S(2)}) %collective-permute-start.5) | collective-permute-done | bytes 327712 | tf_op jit(solution)/shard_map/ppermute | solution.py:12
  81.0 1.5 copy.47
  82.5 2.6 %multiply_add_fusion = f32[32,16,160]{0,2,1:T(8,128)S(1)} fusion(f32[32,16,160]{0,2,1:T(8,128)} %bitcast.63, f32[64,16,160]{0,2,1:T(8,128)} %copy-done.3, f32[32,16]{0,1:T(8,128)S(1)} %get-tuple-element.14, f32[32,16]{0,1:T(8,128)S(1)} %get-tuple-element.13, pred[]{:T(512)S(6)} %eq.44), kind=kLoop, calls=%fused_computation.17 | loop fusion | flops 327680 | bytes 1314817 | tf_op jit(solution)/shard_map/add | solution.py:24
  85.1 1.5 slice_select_fusion
  86.6 1.7 copy.48
  88.3 0.1 multiply_add_fusion.3
  88.4 1.3 collective-permute-done.7
  89.7 1.5 copy.49
  91.2 2.7 %multiply_reduce_fusion.1 = (f32[16]{0:T(128)S(1)}, f32[16,16,160]{0,2,1:T(8,128)S(1)}) fusion(f32[16,16]{0,1:T(8,128)S(1)} %get-tuple-element.9, f32[16,16,160]{0,2,1:T(8,128)} %bitcast.62, f32[16,16]{0,1:T(8,128)S(1)} %get-tuple-element.11, f32[16,16]{0,1:T(8,128)S(1)} %get-tuple-element.10, f32[32,16,160]{0,2,1:T(8,128)} %copy-done.2, pred[]{:T(512)S(6)} %eq.43), kind=kLoop, calls=%fused_computation.15 | loop fusion | flops 368624 | bytes 658497 | tf_op jit(solution)/shard_map/reduce_sum | solution.py:79
  93.9 0.7 convolution_convert_fusion.1
  94.6 0.3 copy-done.6
  95.0 0.3 broadcast_in_dim.13
  95.3 65.7 %all_to_all.10 = bf16[32,16,2560]{2,1,0:T(8,128)(2,1)S(1)} all-to-all(bf16[32,16,2560]{2,1,0:T(8,128)(2,1)S(1)} %bitcast.58), channel_id=1, replica_groups=mesh['groups'=1,'wide'=32] {'wide'}, dimensions={0} | all-to-all | bytes 5242880 | tf_op jit(solution)/shard_map/all_to_all | solution.py:105
  161.0 1.5 copy-done.7
  162.5 2.5 %convolution_bitcast_fusion.2 = f32[512,512]{0,1:T(8,128)} fusion(bf16[512,2560]{1,0:T(8,128)(2,1)S(1)} %bitcast.67, bf16[512,2560]{1,0:T(8,128)(2,1)S(1)} %copy-done.11), kind=kOutput, calls=%fused_computation.12 | convolution fusion | flops 1342177280 | bytes 6291456 | tf_op jit(solution)/shard_map/dot_general | solution.py:108
  165.0 7.3 %convolution_convert_fusion = bf16[512,2560]{1,0:T(8,128)(2,1)} fusion(bf16[512,2560]{1,0:T(8,128)(2,1)S(1)} %copy-done, bf16[512,2560]{1,0:T(8,128)(2,1)} %bitcast.68, bf16[512,2560]{1,0:T(8,128)(2,1)} %param.16, f32[512,512]{0,1:T(8,128)} %convolution_bitcast_fusion.2), kind=kOutput, calls=%fused_computation.1 | convolution fusion | flops 2687238144 | bytes 11534336 | tf_op jit(solution)/shard_map/dot_general | solution.py:115
  172.3 3.8 %all-to-all-start.1 = ((bf16[32,16,2560]{2,1,0:T(8,128)(2,1)}), bf16[32,16,2560]{2,1,0:T(8,128)(2,1)}, u32[]{:S(2)}, u32[]{:S(2)}) async-start(bf16[32,16,2560]{2,1,0:T(8,128)(2,1)} %bitcast.66), calls=%async_computation.1 | async-start | bytes 5242880 | tf_op jit(solution)/shard_map/all_to_all | solution.py:119
  176.2 0.1 copy.53
  176.3 0.1 mul.193
  176.4 1.7 copy.54
  178.1 58.3 %all-to-all-done.1 = bf16[32,16,2560]{2,1,0:T(8,128)(2,1)} async-done(((bf16[32,16,2560]{2,1,0:T(8,128)(2,1)}), bf16[32,16,2560]{2,1,0:T(8,128)(2,1)}, u32[]{:S(2)}, u32[]{:S(2)}) %all-to-all-start.1) | async-done | bytes 2621472 | tf_op jit(solution)/shard_map/all_to_all | solution.py:119
  236.3 3.7 %bitcast_reduce_fusion = bf16[16,16,2560]{2,1,0:T(8,128)(2,1)} fusion(bf16[32,16,2560]{2,1,0:T(8,128)(2,1)} %all-to-all-done.1), kind=kLoop, calls=%fused_computation.3 | loop fusion | flops 655360 | bytes 3932160 | tf_op jit(solution)/shard_map/reduce_sum | solution.py:123
  240.0 3.6 %gather_fusion = bf16[96,2560]{1,0:T(8,128)(2,1)} fusion(bf16[256,2560]{1,0:T(8,128)(2,1)} %bitcast.55, s32[1024]{0:T(1024)S(1)} %pad_clamp_fusion), kind=kCustom, calls=%fused_computation | custom fusion | bytes 983424 | tf_op jit(solution)/shard_map/jit(_take)/gather | solution.py:128
  243.6 1.2 gather.7
  244.8 0.6 multiply_reduce_fusion
  245.4 0.7 add_convert_fusion
  (46 shorter events, 1.0 us)
Async XLA Ops:
  0.0 165.0 %copy-start = (bf16[512,2560]{1,0:T(8,128)(2,1)S(1)}, bf16[512,2560]{1,0:T(8,128)(2,1)}, u32[]{:S(2)}) copy-start(bf16[512,2560]{1,0:T(8,128)(2,1)} %param.17) | copy-start | bytes 7864324
  3.1 1.4 copy-start.5
  4.9 11.3 %collective-permute-start.8 = (f32[128,16]{0,1:T(8,128)S(1)}, f32[128,16]{0,1:T(8,128)S(1)}, u32[]{:S(2)}, u32[]{:S(2)}) collective-permute-start(f32[128,16]{0,1:T(8,128)S(1)} %slice_select_fusion.7), channel_id=1, source_target_pairs={{0,8},{1,9},{2,10},{3,11},{4,12},{5,13},{6,14},{7,15},{8,0},{9,1},... | collective-permute-start | bytes 24584 | tf_op jit(solution)/shard_map/ppermute | solution.py:12
  8.0 8.2 %collective-permute-start = (f32[128,16]{0,1:T(8,128)S(1)}, f32[128,16]{0,1:T(8,128)S(1)}, u32[]{:S(2)}, u32[]{:S(2)}) collective-permute-start(f32[128,16]{0,1:T(8,128)S(1)} %slice_select_fusion.14), channel_id=1, source_target_pairs={{0,8},{1,9},{2,10},{3,11},{4,12},{5,13},{6,14},{7,15},{8,0},{9,1},... | collective-permute-start | bytes 24584 | tf_op jit(solution)/shard_map/ppermute | solution.py:12
  11.6 2.0 copy-start.4
  11.6 3.9 %copy-start.10 = (s32[16,6]{0,1:T(8,128)S(1)}, s32[16,6]{0,1:T(8,128)}, u32[]{:S(2)}) copy-start(s32[16,6]{0,1:T(8,128)} %param.13) | copy-start | bytes 1156
  13.6 30.5 %collective-permute-start.1 = (f32[128,2560]{0,1:T(8,128)}, f32[128,2560]{0,1:T(8,128)}, u32[]{:S(2)}, u32[]{:S(2)}) collective-permute-start(f32[128,2560]{0,1:T(8,128)} %bitcast.5), channel_id=1, source_target_pairs={{0,8},{1,9},{2,10},{3,11},{4,12},{5,13},{6,14},{7,15},{8,0},{9,1},... | collective-permute-start | bytes 3932168 | tf_op jit(solution)/shard_map/ppermute | solution.py:12
  16.3 3.7 %collective-permute-start.2 = (f32[64,16]{0,1:T(8,128)S(1)}, f32[64,16]{0,1:T(8,128)S(1)}, u32[]{:S(2)}, u32[]{:S(2)}) collective-permute-start(f32[64,16]{0,1:T(8,128)S(1)} %slice_select_fusion.12), channel_id=1, source_target_pairs={{0,4},{1,5},{2,6},{3,7},{4,0},{5,1},{6,2},{7,3},{8,12},{9,13},{10,... | collective-permute-start | bytes 12296 | tf_op jit(solution)/shard_map/ppermute | solution.py:12
  17.9 3.7 %collective-permute-start.9 = (f32[64,16]{0,1:T(8,128)S(1)}, f32[64,16]{0,1:T(8,128)S(1)}, u32[]{:S(2)}, u32[]{:S(2)}) collective-permute-start(f32[64,16]{0,1:T(8,128)S(1)} %slice_select_fusion.6), channel_id=1, source_target_pairs={{0,4},{1,5},{2,6},{3,7},{4,0},{5,1},{6,2},{7,3},{8,12},{9,13},{10,... | collective-permute-start | bytes 12296 | tf_op jit(solution)/shard_map/ppermute | solution.py:12
  46.6 1.5 copy-start.1
  49.8 15.4 %collective-permute-start.3 = (f32[64,2560]{1,0:T(8,128)S(1)}, f32[64,2560]{1,0:T(8,128)}, u32[]{:S(2)}, u32[]{:S(2)}) collective-permute-start(f32[64,2560]{1,0:T(8,128)S(1)} %copy.44), channel_id=1, source_target_pairs={{0,4},{1,5},{2,6},{3,7},{4,0},{5,1},{6,2},{7,3},{8,12},{9,13},{10,... | collective-permute-start | bytes 1966088 | tf_op jit(solution)/shard_map/ppermute | solution.py:12
  51.6 3.7 %collective-permute-start.4 = (f32[32,16]{0,1:T(8,128)S(1)}, f32[32,16]{0,1:T(8,128)S(1)}, u32[]{:S(2)}, u32[]{:S(2)}) collective-permute-start(f32[32,16]{0,1:T(8,128)S(1)} %slice_select_fusion.10), channel_id=1, source_target_pairs={{0,2},{1,3},{2,0},{3,1},{4,6},{5,7},{6,4},{7,5},{8,10},{9,11},{10,... | collective-permute-start | bytes 6152 | tf_op jit(solution)/shard_map/ppermute | solution.py:12
  53.1 3.7 %collective-permute-start.10 = (f32[32,16]{0,1:T(8,128)S(1)}, f32[32,16]{0,1:T(8,128)S(1)}, u32[]{:S(2)}, u32[]{:S(2)}) collective-permute-start(f32[32,16]{0,1:T(8,128)S(1)} %slice_select_fusion.5), channel_id=1, source_target_pairs={{0,2},{1,3},{2,0},{3,1},{4,6},{5,7},{6,4},{7,5},{8,10},{9,11},{10,... | collective-permute-start | bytes 6152 | tf_op jit(solution)/shard_map/ppermute | solution.py:12
  70.4 1.5 copy-start.3
  73.6 7.4 %collective-permute-start.5 = (f32[32,2560]{1,0:T(8,128)S(1)}, f32[32,2560]{1,0:T(8,128)S(1)}, u32[]{:S(2)}, u32[]{:S(2)}) collective-permute-start(f32[32,2560]{1,0:T(8,128)S(1)} %copy.46), channel_id=1, source_target_pairs={{0,2},{1,3},{2,0},{3,1},{4,6},{5,7},{6,4},{7,5},{8,10},{9,11},{10,... | collective-permute-start | bytes 983048 | tf_op jit(solution)/shard_map/ppermute | solution.py:12
  75.0 13.3 %collective-permute-start.6 = (f32[16,16]{0,1:T(8,128)S(1)}, f32[16,16]{0,1:T(8,128)S(1)}, u32[]{:S(2)}, u32[]{:S(2)}) collective-permute-start(f32[16,16]{0,1:T(8,128)S(1)} %slice_select_fusion.8), channel_id=1, source_target_pairs={{0,1},{1,0},{2,3},{3,2},{4,5},{5,4},{6,7},{7,6},{8,9},{9,8},{10,11... | collective-permute-start | bytes 3080 | tf_op jit(solution)/shard_map/ppermute | solution.py:12
  75.1 13.2 %collective-permute-start.11 = (f32[16,16]{0,1:T(8,128)S(1)}, f32[16,16]{0,1:T(8,128)S(1)}, u32[]{:S(2)}, u32[]{:S(2)}) collective-permute-start(f32[16,16]{0,1:T(8,128)S(1)} %slice_select_fusion.4), channel_id=1, source_target_pairs={{0,1},{1,0},{2,3},{3,2},{4,5},{5,4},{6,7},{7,6},{8,9},{9,8},{10,11... | collective-permute-start | bytes 3080 | tf_op jit(solution)/shard_map/ppermute | solution.py:12
  85.1 1.5 copy-start.2
  88.3 1.4 collective-permute-start.7
  91.2 2.7 %copy-start.9 = (f32[2560]{0:T(1024)S(1)}, f32[2560]{0:T(1024)}, u32[]{:S(2)}) copy-start(f32[2560]{0:T(1024)} %param.12) | copy-start | bytes 30724
  93.8 1.1 copy-start.6
  95.3 67.2 %copy-start.11 = (bf16[512,2560]{1,0:T(8,128)(2,1)S(1)}, bf16[512,2560]{1,0:T(8,128)(2,1)}, u32[]{:S(2)}) copy-start(bf16[512,2560]{1,0:T(8,128)(2,1)} %param.15) | copy-start | bytes 7864324
  161.0 1.5 copy-start.7
  172.3 3.8 %copy-start.8 = (s32[16,6]{0,1:T(8,128)S(1)}, s32[16,6]{0,1:T(8,128)}, u32[]{:S(2)}) copy-start(s32[16,6]{0,1:T(8,128)} %param.14) | copy-start | bytes 1156
  172.3 64.0 %all-to-all-start.1 = ((bf16[32,16,2560]{2,1,0:T(8,128)(2,1)}), bf16[32,16,2560]{2,1,0:T(8,128)(2,1)}, u32[]{:S(2)}, u32[]{:S(2)}) async-start(bf16[32,16,2560]{2,1,0:T(8,128)(2,1)} %bitcast.66), calls=%async_computation.1 | async-start | bytes 5242880 | tf_op jit(solution)/shard_map/all_to_all | solution.py:119
where the time goes:
time: 247 us; the launch traced here: 246 us
  waiting for transfers between devices  102 us (41%)
  blocking collectives  65.7 us (27%)
  local copies, waits for them, and re-layouts  25.8 us (10%)
  other arithmetic  22.6 us (9%)
  starting transfers between devices  16.6 us (7%)
  matrix products  13.2 us (5%)
    all_to_all x1, blocking collectives, on_device(): lax.all_to_all(sent_rows, 'wide', split_axis=0, concat_axis=0, tiled=True)  65.7 us
    all_to_all x1, waiting for transfers between devices, on_device(): lax.all_to_all(partial_value.astype(jnp.bfloat16), 'wide', split_axis=0,...  58.3 us
    ppermute x12, waiting for transfers between devices, partner(): return lax.ppermute(value, axis, pairs)  43.6 us
    ppermute x12, starting transfers between devices, partner(): return lax.ppermute(value, axis, pairs)  12.7 us
    unnamed x28, local copies, waits for them, and re-layouts  7.97 us
    add x3, other arithmetic, merge_partials(): summed + sum_second.reshape(row_count, head_count, -1) * factor_second[:,...  7.6 us
    dot_general x1, matrix products, on_device(): lax.dot_general(hidden, w_down, (((0,), (0,)), ((), ())), preferred_eleme...  7.29 us
    select_n x4, other arithmetic, on_device(): sent_sum = jnp.where(upper_half, summed[:half_rows], summed[half_rows:])  5.86 us
  transfers between devices with their start and end apart: 13, of which 9 were waited for; matrix products, arithmetic and copies ran while one was open for 6% of the time, Pallas kernels for 0%

commit v1 on v0

v1 whole, which is shorter than its diff:
```python
import functools

import jax
import jax.numpy as jnp
from jax import lax
from jax.experimental import pallas as pl
from jax.experimental.pallas import tpu as pltpu
from jax.sharding import PartitionSpec as P

HEADS = 16
LANES = 128
F32 = jnp.float32
BF16 = jnp.bfloat16


def kernel(
    devices,
    q_ref, k_ref, v_ref, gain_ref, re_ref, rw_ref, wg_hbm, wu_hbm, wd_hbm,
    out_ref,
    kvp, kvr, s_scr, p_scr, tot_scr, gath, proj, own_rows, gates, wg, wu, wd,
    pa, pb, r1a, r1b, r2a, r2b, r3a, r3b, ua, ub, r4a, r4b,
    w_sem, a_send, a_recv, g_send, g_recv,
    s1_send, s1_recv, s2_send, s2_recv, s3_send, s3_recv, s4_send, s4_recv,
):
    me = lax.axis_index("wide")
    group = HEADS
    spot = lax.rem(me, group)
    base = me - spot
    depth = devices // 8
    core = lax.rem(me, 2)
    xi = lax.rem(me // 2, 2)
    yi = lax.rem(me // 4, 2)
    zi = me // 8
    n_q = q_ref.shape[0]
    width = v_ref.shape[1]
    patches = k_ref.shape[0]
    key_size = k_ref.shape[1] // HEADS
    value_size = width // HEADS
    extra = value_size - LANES
    pieces = LANES // extra
    half_w = width // 2
    rows_dev = re_ref.shape[0]
    wide_kv = kvp.shape[2]

    def dev(z, y, x, c):
        return z * 8 + y * 4 + x * 2 + c

    sib = dev(zi, yi, xi, 1 - core)
    xn = dev(zi, yi, 1 - xi, core)
    yn = dev(zi, 1 - yi, xi, core)

    def rcopy(src, dst, ssem, rsem, target):
        return pltpu.make_async_remote_copy(
            src_ref=src, dst_ref=dst, send_sem=ssem, recv_sem=rsem,
            device_id={"wide": target}, device_id_type=pl.DeviceIdType.MESH,
        )

    barrier = pltpu.get_barrier_semaphore()
    per_group = group // 8
    for k in range(1, group):
        pl.semaphore_signal(
            barrier, inc=1, device_id={"wide": base + lax.rem(spot + k, group)},
            device_id_type=pl.DeviceIdType.MESH,
        )
    far = depth - per_group
    z_base = zi // per_group * per_group
    for k in range(far):
        zt = lax.rem(z_base + per_group + k, depth)
        pl.semaphore_signal(
            barrier, inc=1, device_id={"wide": dev(zt, yi, xi, core)},
            device_id_type=pl.DeviceIdType.MESH,
        )

    w_copies = [
        pltpu.make_async_copy(wg_hbm, wg, w_sem.at[0]),
        pltpu.make_async_copy(wu_hbm, wu, w_sem.at[1]),
        pltpu.make_async_copy(wd_hbm, wd, w_sem.at[2]),
    ]

    pad = jnp.zeros((patches, wide_kv - value_size - key_size), BF16)
    for h in range(HEADS):
        kvp[h] = jnp.concatenate(
            [
                v_ref[:, h * value_size : (h + 1) * value_size],
                k_ref[:, h * key_size : (h + 1) * key_size],
                pad,
            ],
            axis=1,
        )
    pl.semaphore_wait(barrier, group - 1 + far)

    def a2a(k):
        t = lax.rem(spot + k, group)
        return rcopy(kvp.at[t], kvr.at[spot], a_send.at[k], a_recv.at[k], base + t)

    def a2a_in(k):
        s = lax.rem(spot + group - k, group)
        return rcopy(kvp.at[s], kvr.at[s], a_send.at[k], a_recv.at[k], base + s)

    def send_kv(k, carry):
        a2a(k).start()
        return carry

    lax.fori_loop(1, group, send_kv, 0)
    for c in w_copies:
        c.start()
    kvr[spot] = kvp[spot]

    q_head = jnp.zeros((n_q, key_size), F32)
    for h in range(HEADS):
        q_head = jnp.where(
            spot == h, q_ref[:, h * key_size : (h + 1) * key_size].astype(F32), q_head
        )
    q_pad = jnp.concatenate(
        [
            jnp.zeros((n_q, value_size), F32),
            q_head,
            jnp.zeros((n_q, wide_kv - value_size - key_size), F32),
        ],
        axis=1,
    ).astype(BF16)

    shares = rw_ref[...].astype(F32)
    shares = shares / jnp.sum(shares, axis=1, keepdims=True)
    lane = lax.broadcasted_iota(jnp.int32, (rows_dev, LANES), 1)
    table = jnp.zeros((rows_dev, LANES), F32)
    for k in range(re_ref.shape[1]):
        table = table + jnp.where(re_ref[:, k : k + 1] == lane, shares[:, k : k + 1], 0.0)
    table_hi = table.astype(BF16)
    table_lo = (table - table_hi.astype(F32)).astype(BF16)

    def wait_kv(k, carry):
        a2a_in(k).wait_recv()
        return carry

    lax.fori_loop(1, group, wait_kv, 0)

    scale = key_size ** (-0.5)
    for s in range(group):
        s_scr[:, s * patches : (s + 1) * patches] = (
            lax.dot_general(
                q_pad, kvr[s], (((1,), (1,)), ((), ())), preferred_element_type=F32
            )
            * scale
        )

    step = 32

    def soft(r, carry):
        rows = pl.ds(pl.multiple_of(r * step, step), step)
        s = s_scr[rows, :]
        p = jnp.exp(s - jnp.max(s, axis=1, keepdims=True))
        tot_scr[rows, :] = jnp.broadcast_to(jnp.sum(p, axis=1, keepdims=True), (step, LANES))
        p_scr[rows, :] = p.astype(BF16)
        return carry

    lax.fori_loop(0, n_q // step, soft, 0)
    acc = jnp.zeros((n_q, wide_kv), F32)
    for s in range(group):
        acc = acc + jnp.dot(
            p_scr[:, s * patches : (s + 1) * patches], kvr[s], preferred_element_type=F32
        )
    att = (acc / tot_scr[:, 0:1]).astype(BF16)
    main = n_q
    part = n_q // pieces
    gath[me, 0:main, :] = att[:, :LANES]
    gath[me, main : main + part, :] = jnp.concatenate(
        [att[g * part : (g + 1) * part, LANES : LANES + extra] for g in range(pieces)], axis=1
    )
    gath[me, main + part : main + part + rows_dev, :] = table_hi
    gath[me, main + part + rows_dev : main + part + 2 * rows_dev, :] = table_lo

    tall = main + part + 2 * rows_dev
    half = tall // 2
    top, low = pl.ds(0, half), pl.ds(half, half)

    def src_z(dz):
        return lax.rem(zi + depth - dz, depth)

    def own(dz):
        return dev(src_z(dz), yi, xi, core)

    def blk_x(dz):
        return dev(src_z(dz), yi, 1 - xi, core)

    def blk_y(dz):
        return dev(src_z(dz), 1 - yi, xi, core)

    def blk_d(dz):
        return dev(src_z(dz), 1 - yi, 1 - xi, core)

    def gcopy(kind, dz, block, target, rows=None):
        ref = gath.at[block] if rows is None else gath.at[block, rows]
        return rcopy(ref, ref, g_send.at[kind, dz], g_recv.at[kind, dz], target)

    def z_out(dz):
        zt = lax.rem(zi + dz, depth)
        return gcopy(0, dz, me, dev(zt, yi, xi, core))

    def send_z(dz, carry):
        z_out(dz).start()
        return carry

    lax.fori_loop(1, depth, send_z, 0)

    def spread(dz):
        gcopy(1, dz, own(dz), xn).start()
        gcopy(2, dz, own(dz), yn).start()
        gcopy(3, dz, own(dz), sib).start()

    spread(0)

    def spread_z(dz, carry):
        gcopy(0, dz, own(dz), me).wait_recv()
        spread(dz)
        return carry

    lax.fori_loop(1, depth, spread_z, 0)

    def onward(dz, carry):
        gcopy(1, dz, blk_x(dz), xn).wait_recv()
        gcopy(4, dz, blk_x(dz), yn, top).start()
        gcopy(5, dz, blk_x(dz), sib).start()
        gcopy(2, dz, blk_y(dz), yn).wait_recv()
        gcopy(6, dz, blk_y(dz), xn, low).start()
        gcopy(7, dz, blk_y(dz), sib).start()
        return carry

    lax.fori_loop(0, depth, onward, 0)

    def last(dz, carry):
        gcopy(4, dz, blk_d(dz), yn, top).wait_recv()
        gcopy(6, dz, blk_d(dz), xn, low).wait_recv()
        gcopy(8, dz, blk_d(dz), sib).start()
        return carry

    lax.fori_loop(0, depth, last, 0)

    def other(block):
        return block + 1 - 2 * core

    def from_sib(dz, carry):
        gcopy(3, dz, other(own(dz)), sib).wait_recv()
        gcopy(5, dz, other(blk_x(dz)), sib).wait_recv()
        gcopy(7, dz, other(blk_y(dz)), sib).wait_recv()
        gcopy(8, dz, other(blk_d(dz)), sib).wait_recv()
        return carry

    lax.fori_loop(0, depth, from_sib, 0)

    images = devices // group
    quads = HEADS // pieces

    def lay(it, carry):
        image, quad = it // quads, lax.rem(it, quads)
        first = image * group + quad * pieces
        cols = []
        for g in range(pieces):
            tail = gath[first + g, main : main + part, :]
            cols.append(gath[first + g, 0:main, :])
            cols.append(
                jnp.concatenate(
                    [tail[:, i * extra : (i + 1) * extra] for i in range(pieces)], axis=0
                )
            )
        span = pieces * value_size
        proj[
            pl.ds(pl.multiple_of(image * n_q, n_q), n_q),
            pl.ds(pl.multiple_of(quad * span, LANES), span),
        ] = jnp.concatenate(cols, axis=1)
        return carry

    lax.fori_loop(0, images * quads, lay, 0)

    own_rows[...] = proj[pl.ds(pl.multiple_of(me * rows_dev, rows_dev), rows_dev), :]
    expert = me // 2
    lane_row = lax.broadcasted_iota(jnp.int32, (rows_dev, LANES), 1)

    def norm_rows(d, carry):
        rows = pl.ds(pl.multiple_of(d * rows_dev, rows_dev), rows_dev)
        x = proj[rows, :].astype(F32)
        r = lax.rsqrt(jnp.mean(x * x, axis=1, keepdims=True) + 1e-06)
        proj[rows, :] = (x * r * gain_ref[...]).astype(BF16)
        share = gath[d, main + part : main + part + rows_dev, :].astype(F32) + gath[
            d, main + part + rows_dev : main + part + 2 * rows_dev, :
        ].astype(F32)
        mine = jnp.sum(jnp.where(lane_row == expert, share, 0.0), axis=1, keepdims=True)
        gates[rows, :] = jnp.broadcast_to(mine, (rows_dev, LANES))
        return carry

    lax.fori_loop(0, devices, norm_rows, 0)
    for c in w_copies:
        c.wait()

    block_rows = n_q
    z_block = block_rows // (8 * rows_dev)

    def s1(z, side):
        src = pa if side == 0 else pb
        dst = r1a if side == 0 else r1b
        return rcopy(
            src.at[1 - core, :, z], dst.at[:, z], s1_send.at[side, z], s1_recv.at[side, z], sib
        )

    def experts(r, carry):
        rows = pl.ds(pl.multiple_of(r * block_rows, block_rows), block_rows)
        x = proj[rows, :]
        dims = (((1,), (1,)), ((), ()))
        g = lax.dot_general(x, wg[...], dims, preferred_element_type=F32)
        u = lax.dot_general(x, wu[...], dims, preferred_element_type=F32)
        hidden = (g / (1.0 + jnp.exp(-g)) * u).astype(BF16)
        share = gates[rows, 0:1]
        chunk = half_w // 2
        for n in range(4):
            y = jnp.dot(
                hidden, wd[:, n * chunk : (n + 1) * chunk], preferred_element_type=F32
            )
            y = (y * share).astype(BF16)
            cols = slice((n % 2) * chunk, (n % 2 + 1) * chunk)
            for j in range(8 * z_block):
                c, x_, y_, z = j % 2, j // 2 % 2, j // 4 % 2, j // 8
                piece = y[j * rows_dev : (j + 1) * rows_dev]
                if n < 2:
                    pa[c, x_, r * z_block + z, y_, :, cols] = piece
                else:
                    pb[c, y_, r * z_block + z, x_, :, cols] = piece
        for z in range(z_block):
            s1(r * z_block + z, 0).start()
            s1(r * z_block + z, 1).start()
        return carry

    lax.fori_loop(0, devices * rows_dev // block_rows, experts, 0)

    def add_into(dst, d_ix, others):
        total = dst[d_ix].astype(F32)
        for ref, ix in others:
            total = total + ref[ix].astype(F32)
        return total.astype(BF16)

    def s2a(z):
        return rcopy(pa.at[core, 1 - xi, z], r2a.at[z], s2_send.at[0, z], s2_recv.at[0, z], xn)

    def s2b(z):
        return rcopy(pb.at[core, 1 - yi, z], r2b.at[z], s2_send.at[1, z], s2_recv.at[1, z], yn)

    def home1(z, carry):
        s1(z, 0).wait_recv()
        pa[core, 1 - xi, z] = add_into(pa, (core, 1 - xi, z), [(r1a, (1 - xi, z))])
        s2a(z).start()
        s1(z, 1).wait_recv()
        pb[core, 1 - yi, z] = add_into(pb, (core, 1 - yi, z), [(r1b, (1 - yi, z))])
        s2b(z).start()
        return carry

    lax.fori_loop(0, depth, home1, 0)

    def s3a(z):
        return rcopy(
            pa.at[core, xi, z, 1 - yi], r3a.at[z], s3_send.at[0, z], s3_recv.at[0, z], yn
        )

    def s3b(z):
        return rcopy(
            pb.at[core, yi, z, 1 - xi], r3b.at[z], s3_send.at[1, z], s3_recv.at[1, z], xn
        )

    def home2(z, carry):
        s2a(z).wait_recv()
        pa[core, xi, z] = add_into(pa, (core, xi, z), [(r1a, (xi, z)), (r2a, z)])
        s3a(z).start()
        s2b(z).wait_recv()
        pb[core, yi, z] = add_into(pb, (core, yi, z), [(r1b, (yi, z)), (r2b, z)])
        s3b(z).start()
        return carry

    lax.fori_loop(0, depth, home2, 0)

    def s4(dz, side):
        zt = lax.rem(zi + dz, depth)
        src = ua if side == 0 else ub
        dst = r4a if side == 0 else r4b
        return rcopy(
            src.at[zt], dst.at[dz], s4_send.at[side, dz], s4_recv.at[side, dz],
            dev(zt, yi, xi, core),
        )

    def home3(dz, carry):
        z = lax.rem(zi + dz, depth)
        s3a(z).wait_recv()
        ua[z] = add_into(pa, (core, xi, z, yi), [(r3a, z)])
        s3b(z).wait_recv()
        ub[z] = add_into(pb, (core, yi, z, xi), [(r3b, z)])

        @pl.when(dz > 0)
        def _():
            s4(dz, 0).start()
            s4(dz, 1).start()

        return carry

    def far_first(i, carry):
        return home3(depth - 1 - i, carry)

    lax.fori_loop(0, depth, far_first, 0)
    mine = own_rows[...].astype(F32)
    sum_a = mine[:, :half_w] + ua[zi].astype(F32)
    sum_b = mine[:, half_w:] + ub[zi].astype(F32)

    def home4(dz, carry):
        left, right = carry
        s4(dz, 0).wait_recv()
        s4(dz, 1).wait_recv()
        return left + r4a[dz].astype(F32), right + r4b[dz].astype(F32)

    sum_a, sum_b = lax.fori_loop(1, depth, home4, (sum_a, sum_b))
    out_ref[:, :half_w] = sum_a.astype(BF16)
    out_ref[:, half_w:] = sum_b.astype(BF16)

    def sent_kv(k, carry):
        a2a(k).wait_send()
        return carry

    lax.fori_loop(1, group, sent_kv, 0)

    def sent_z(dz, carry):
        z_out(dz).wait_send()
        s4(dz, 0).wait_send()
        s4(dz, 1).wait_send()
        return carry

    lax.fori_loop(1, depth, sent_z, 0)

    def sent(dz, carry):
        gcopy(1, dz, own(dz), xn).wait_send()
        gcopy(2, dz, own(dz), yn).wait_send()
        gcopy(3, dz, own(dz), sib).wait_send()
        gcopy(4, dz, blk_x(dz), yn, top).wait_send()
        gcopy(5, dz, blk_x(dz), sib).wait_send()
        gcopy(6, dz, blk_y(dz), xn, low).wait_send()
        gcopy(7, dz, blk_y(dz), sib).wait_send()
        gcopy(8, dz, blk_d(dz), sib).wait_send()
        for copy in (s1(dz, 0), s1(dz, 1), s2a(dz), s2b(dz), s3a(dz), s3b(dz)):
            copy.wait_send()
        return carry

    lax.fori_loop(0, depth, sent, 0)


def on_device(
    queries, patch_keys, patch_values, norm_gain, route_experts, route_weights, w_gate, w_up, w_down
):
    devices = lax.axis_size("wide")
    n_q = queries.shape[0]
    patches, vision = patch_keys.shape
    width = patch_values.shape[1]
    rows_dev = route_experts.shape[0]
    hidden = w_gate.shape[0]
    depth = devices // 8
    group = HEADS
    assert n_q == rows_dev * group and n_q % (8 * rows_dev) == 0 and depth % 2 == 0
    value_size = width // HEADS
    extra = value_size - LANES
    pieces = LANES // extra
    wide_kv = -(-(value_size + vision // HEADS) // LANES) * LANES
    tall = n_q + n_q // pieces + 2 * rows_dev
    rows = devices * rows_dev
    half = width // 2
    vm = pltpu.VMEM
    dma = pltpu.SemaphoreType.DMA
    scratch = [
        vm((group, patches, wide_kv), BF16),
        vm((group, patches, wide_kv), BF16),
        vm((n_q, group * patches), F32),
        vm((n_q, group * patches), BF16),
        vm((n_q, LANES), F32),
        vm((devices, tall, LANES), BF16),
        vm((rows, width), BF16),
        vm((rows_dev, width), BF16),
        vm((rows, LANES), F32),
        vm((hidden, width), BF16),
        vm((hidden, width), BF16),
        vm((hidden, width), BF16),
        vm((2, 2, depth, 2, rows_dev, half), BF16),
        vm((2, 2, depth, 2, rows_dev, half), BF16),
        vm((2, depth, 2, rows_dev, half), BF16),
        vm((2, depth, 2, rows_dev, half), BF16),
        vm((depth, 2, rows_dev, half), BF16),
        vm((depth, 2, rows_dev, half), BF16),
        vm((depth, rows_dev, half), BF16),
        vm((depth, rows_dev, half), BF16),
        vm((depth, rows_dev, half), BF16),
        vm((depth, rows_dev, half), BF16),
        vm((depth, rows_dev, half), BF16),
        vm((depth, rows_dev, half), BF16),
        dma((3,)),
        dma((group,)), dma((group,)),
        dma((9, depth)), dma((9, depth)),
        dma((2, depth)), dma((2, depth)),
        dma((2, depth)), dma((2, depth)),
        dma((2, depth)), dma((2, depth)),
        dma((2, depth)), dma((2, depth)),
    ]
    vspec = pl.BlockSpec(memory_space=pltpu.VMEM)
    hspec = pl.BlockSpec(memory_space=pl.ANY)
    return pl.pallas_call(
        functools.partial(kernel, devices),
        out_shape=jax.ShapeDtypeStruct((rows_dev, width), BF16),
        in_specs=[vspec] * 6 + [hspec] * 3,
        out_specs=vspec,
        scratch_shapes=scratch,
        compiler_params=pltpu.CompilerParams(
            collective_id=0, has_side_effects=True, vmem_limit_bytes=62 * 1024 * 1024
        ),
    )(
        queries, patch_keys, patch_values, norm_gain.reshape(1, -1), route_experts, route_weights,
        w_gate, w_up, w_down,
    )


def solution(mesh):
    rows = P(("groups", "wide"), None)
    return jax.shard_map(
        on_device,
        mesh=mesh,
        in_specs=(
            P("groups", None), rows, rows, P(), rows, rows,
            P("wide", None), P("wide", None), P("wide", None),
        ),
        out_specs=rows,
        check_vma=False,
    )
```

time: 247 us -> 86 us (0.35)
  waiting for transfers between devices: 102 us -> 0 us
  Pallas kernels: 0 us -> 80.1 us
  blocking collectives: 65.7 us -> 0 us
  other arithmetic: 22.6 us -> 0 us
  local copies, waits for them, and re-layouts: 25.8 us -> 5.56 us
  starting transfers between devices: 16.6 us -> 0 us
  matrix products: 13.2 us -> 0 us
    pallas_call x0 -> x1, Pallas kernels: none -> 80.1 us  [on_device(): pl.pallas_call(functools.partial(kernel, devices), out_shape=jax.ShapeDty...]
    all_to_all x1 -> x0, blocking collectives: 65.7 us -> none  [on_device(): lax.all_to_all(sent_rows, 'wide', split_axis=0, concat_axis=0, tiled=True)]
    all_to_all x1 -> x0, waiting for transfers between devices: 58.3 us -> none  [on_device(): lax.all_to_all(partial_value.astype(jnp.bfloat16), 'wide', split_axis=0,...]
    ppermute x12 -> x0, waiting for transfers between devices: 43.6 us -> none  [partner(): return lax.ppermute(value, axis, pairs)]
    dot_general x5 -> x0, matrix products: 13.2 us -> none  [the longest x1 7.29 us: on_device(): lax.dot_general(hidden, w_down, (((0,), (0,)), ((), ())), preferred_eleme...]
    ppermute x12 -> x0, starting transfers between devices: 12.7 us -> none  [partner(): return lax.ppermute(value, axis, pairs)]
    add x7 -> x0, other arithmetic: 7.87 us -> none  [the longest x3 7.6 us: merge_partials(): summed + sum_second.reshape(row_count, head_count, -1) * factor_second[:,...]
    reduce_sum x6 -> x0, other arithmetic: 7.45 us -> none  [the longest x1 3.68 us: on_device(): jnp.sum(returned.reshape(experts, 2, -1, model_width), axis=1)]
  transfers between devices with their start and end apart: 13 -> 0, of which waited for: 9 -> 0; matrix products, arithmetic and copies ran while one was open for 6% -> 0% of each run, Pallas kernels for 0% -> 0%
where the time goes in v1:
time: 86 us; the launch traced here: 85.7 us
  Pallas kernels  80.1 us (93%)
  local copies, waits for them, and re-layouts  5.56 us (6%)
    pallas_call x1, Pallas kernels, on_device(): pl.pallas_call(functools.partial(kernel, devices), out_shape=jax.ShapeDty...  80.1 us
    unnamed x3, local copies, waits for them, and re-layouts  4.24 us

profile of v1, /device:TPU:0, one launch (start us, length us, event | category | flops | bytes accessed | tf_op | source)
XLA Modules:
  0.0 85.7 jit_solution(189956514417633718)
XLA Ops:
  0.0 1.4 %copy.10.re_ref = s32[16,6]{1,0:T(8,128)} copy(s32[16,6]{0,1:T(8,128)} %param.13) | data formatting | bytes 768 | tf_op args[4]
  1.4 1.4 %copy.11.rw_ref = s32[16,6]{1,0:T(8,128)} copy(s32[16,6]{0,1:T(8,128)} %param.14) | data formatting | bytes 768 | tf_op args[5]
  2.7 1.3 %reshape.3.gain_ref = f32[1,2560]{1,0:T(1,128)} reshape(f32[2560]{0:T(1024)} %param.12) | data formatting | bytes 20480 | tf_op jit(solution)/shard_map/reshape | solution.py:515
  4.0 80.1 %shard_map.91 = bf16[16,2560]{1,0:T(8,128)(2,1)} custom-call(bf16[256,1152]{1,0:T(8,128)(2,1)} %q_ref.1, bf16[128,1152]{1,0:T(8,128)(2,1)} %k_ref.1, bf16[128,2560]{1,0:T(8,128)(2,1)} %v_ref.1, f32[1,2560]{1,0:T(1,128)} %reshape.3.gain_ref, s32[16,6]{1,0:T(8,128)} %copy.10.re_ref, s32[16,6]{1,0:T(8,128)} %copy.11.rw_ref, bf16[512,2560]{1,0:T(8,128)(2,1)} %wg_hbm.1, ...), custom_call_target="tpu_custom_call" | custom-call | tf_op jit(solution)/shard_map/pallas_call | solution.py:505
  84.2 1.5 %copy.13 = bf16[16,2560]{1,0:T(8,128)(2,1)} copy(bf16[16,2560]{1,0:T(8,128)(2,1)} %shard_map.91) | data formatting | bytes 163840

commit v2 on v1

--- a/solution.py
+++ b/solution.py
@@ -15,9 +15,9 @@
 
 def kernel(
     devices,
-    q_ref, k_ref, v_ref, gain_ref, re_ref, rw_ref, wg_hbm, wu_hbm, wd_hbm,
+    q_hbm, k_hbm, v_hbm, gain_ref, re_ref, rw_ref, wg_hbm, wu_hbm, wd_hbm,
     out_ref,
-    kvp, kvr, s_scr, p_scr, tot_scr, gath, proj, own_rows, gates, wg, wu, wd,
+    q_ref, k_ref, v_ref, kvp, kvr, s_scr, p_scr, tot_scr, gath, proj, own_rows, gates, wg, wu, wd,
     pa, pb, r1a, r1b, r2a, r2b, r3a, r3b, ua, ub, r4a, r4b,
     w_sem, a_send, a_recv, g_send, g_recv,
     s1_send, s1_recv, s2_send, s2_recv, s3_send, s3_recv, s4_send, s4_recv,
@@ -39,7 +39,7 @@
     extra = value_size - LANES
     pieces = LANES // extra
     half_w = width // 2
-    rows_dev = re_ref.shape[0]
+    rows_dev = re_ref.shape[1]
     wide_kv = kvp.shape[2]
 
     def dev(z, y, x, c):
@@ -76,6 +76,15 @@
         pltpu.make_async_copy(wu_hbm, wu, w_sem.at[1]),
         pltpu.make_async_copy(wd_hbm, wd, w_sem.at[2]),
     ]
+    in_copies = [
+        pltpu.make_async_copy(k_hbm, k_ref, w_sem.at[3]),
+        pltpu.make_async_copy(v_hbm, v_ref, w_sem.at[4]),
+        pltpu.make_async_copy(q_hbm, q_ref, w_sem.at[5]),
+    ]
+    for c in in_copies:
+        c.start()
+    for c in in_copies:
+        c.wait()
 
     pad = jnp.zeros((patches, wide_kv - value_size - key_size), BF16)
     for h in range(HEADS):
@@ -121,13 +130,16 @@
     ).astype(BF16)
 
     shares = rw_ref[...].astype(F32)
-    shares = shares / jnp.sum(shares, axis=1, keepdims=True)
+    shares = shares / jnp.sum(shares, axis=0, keepdims=True)
+    split = LANES // 2
+    line = lax.rem(lax.broadcasted_iota(jnp.int32, (LANES, rows_dev), 0), split)
+    table = jnp.zeros((LANES, rows_dev), F32)
+    for k in range(re_ref.shape[0]):
+        table = table + jnp.where(re_ref[k : k + 1, :] == line, shares[k : k + 1, :], 0.0)
+    table = jnp.concatenate([table, jnp.zeros((LANES, LANES - rows_dev), F32)], axis=1).T[:rows_dev]
     lane = lax.broadcasted_iota(jnp.int32, (rows_dev, LANES), 1)
-    table = jnp.zeros((rows_dev, LANES), F32)
-    for k in range(re_ref.shape[1]):
-        table = table + jnp.where(re_ref[:, k : k + 1] == lane, shares[:, k : k + 1], 0.0)
-    table_hi = table.astype(BF16)
-    table_lo = (table - table_hi.astype(F32)).astype(BF16)
+    table_hi = table.astype(BF16).astype(F32)
+    table = jnp.where(lane < split, table_hi, table - table_hi).astype(BF16)
 
     def wait_kv(k, carry):
         a2a_in(k).wait_recv()
@@ -167,92 +179,94 @@
     gath[me, main : main + part, :] = jnp.concatenate(
         [att[g * part : (g + 1) * part, LANES : LANES + extra] for g in range(pieces)], axis=1
     )
-    gath[me, main + part : main + part + rows_dev, :] = table_hi
-    gath[me, main + part + rows_dev : main + part + 2 * rows_dev, :] = table_lo
-
-    tall = main + part + 2 * rows_dev
-    half = tall // 2
-    top, low = pl.ds(0, half), pl.ds(half, half)
-
-    def src_z(dz):
-        return lax.rem(zi + depth - dz, depth)
-
-    def own(dz):
-        return dev(src_z(dz), yi, xi, core)
-
-    def blk_x(dz):
-        return dev(src_z(dz), yi, 1 - xi, core)
-
-    def blk_y(dz):
-        return dev(src_z(dz), 1 - yi, xi, core)
-
-    def blk_d(dz):
-        return dev(src_z(dz), 1 - yi, 1 - xi, core)
-
-    def gcopy(kind, dz, block, target, rows=None):
+    gath[me, main + part : main + part + rows_dev, :] = table
+
+    tall = main + part + rows_dev
+    half = tall // 32 * 16
+    top, low = pl.ds(0, half), pl.ds(half, tall - half)
+
+    def zo(i):
+        near = z_base + lax.rem(lax.rem(zi, per_group) + i, per_group)
+        return jnp.where(i < per_group, near, lax.rem(z_base + i, depth))
+
+    def own(z):
+        return dev(z, yi, xi, core)
+
+    def blk_x(z):
+        return dev(z, yi, 1 - xi, core)
+
+    def blk_y(z):
+        return dev(z, 1 - yi, xi, core)
+
+    def blk_d(z):
+        return dev(z, 1 - yi, 1 - xi, core)
+
+    def gcopy(kind, z, block, target, rows=None):
         ref = gath.at[block] if rows is None else gath.at[block, rows]
-        return rcopy(ref, ref, g_send.at[kind, dz], g_recv.at[kind, dz], target)
-
-    def z_out(dz):
-        zt = lax.rem(zi + dz, depth)
-        return gcopy(0, dz, me, dev(zt, yi, xi, core))
-
-    def send_z(dz, carry):
-        z_out(dz).start()
+        return rcopy(ref, ref, g_send.at[kind, z], g_recv.at[kind, z], target)
+
+    def z_out(i):
+        zt = zo(i)
+        ref = gath.at[me]
+        return rcopy(ref, ref, g_send.at[0, zt], g_recv.at[0, zi], own(zt))
+
+    def send_z(i, carry):
+        z_out(i).start()
         return carry
 
     lax.fori_loop(1, depth, send_z, 0)
 
-    def spread(dz):
-        gcopy(1, dz, own(dz), xn).start()
-        gcopy(2, dz, own(dz), yn).start()
-        gcopy(3, dz, own(dz), sib).start()
-
-    spread(0)
-
-    def spread_z(dz, carry):
-        gcopy(0, dz, own(dz), me).wait_recv()
-        spread(dz)
-        return carry
-
-    lax.fori_loop(1, depth, spread_z, 0)
-
-    def onward(dz, carry):
-        gcopy(1, dz, blk_x(dz), xn).wait_recv()
-        gcopy(4, dz, blk_x(dz), yn, top).start()
-        gcopy(5, dz, blk_x(dz), sib).start()
-        gcopy(2, dz, blk_y(dz), yn).wait_recv()
-        gcopy(6, dz, blk_y(dz), xn, low).start()
-        gcopy(7, dz, blk_y(dz), sib).start()
-        return carry
-
-    lax.fori_loop(0, depth, onward, 0)
-
-    def last(dz, carry):
-        gcopy(4, dz, blk_d(dz), yn, top).wait_recv()
-        gcopy(6, dz, blk_d(dz), xn, low).wait_recv()
-        gcopy(8, dz, blk_d(dz), sib).start()
-        return carry
-
-    lax.fori_loop(0, depth, last, 0)
+    def spread(z):
+        gcopy(1, z, own(z), xn).start()
+        gcopy(2, z, own(z), yn).start()
+        gcopy(3, z, own(z), sib).start()
+
+    spread(zi)
+
+    def spread_z(i, carry):
+        gcopy(0, zo(i), own(zo(i)), own(zo(i))).wait_recv()
+        spread(zo(i))
+        return carry
+
+    lax.fori_loop(1, per_group, spread_z, 0)
+
+    def onward(i, carry):
+        z = zo(i)
+        gcopy(1, z, blk_x(z), xn).wait_recv()
+        gcopy(4, z, blk_x(z), yn, top).start()
+        gcopy(5, z, blk_x(z), sib).start()
+        gcopy(2, z, blk_y(z), yn).wait_recv()
+        gcopy(6, z, blk_y(z), xn, low).start()
+        gcopy(7, z, blk_y(z), sib).start()
+        return carry
+
+    def last(i, carry):
+        z = zo(i)
+        gcopy(4, z, blk_d(z), yn, top).wait_recv()
+        gcopy(6, z, blk_d(z), xn, low).wait_recv()
+        gcopy(8, z, blk_d(z), sib).start()
+        return carry
 
     def other(block):
         return block + 1 - 2 * core
 
-    def from_sib(dz, carry):
-        gcopy(3, dz, other(own(dz)), sib).wait_recv()
-        gcopy(5, dz, other(blk_x(dz)), sib).wait_recv()
-        gcopy(7, dz, other(blk_y(dz)), sib).wait_recv()
-        gcopy(8, dz, other(blk_d(dz)), sib).wait_recv()
-        return carry
-
-    lax.fori_loop(0, depth, from_sib, 0)
+    def from_sib(i, carry):
+        z = zo(i)
+        gcopy(3, z, other(own(z)), sib).wait_recv()
+        gcopy(5, z, other(blk_x(z)), sib).wait_recv()
+        gcopy(7, z, other(blk_y(z)), sib).wait_recv()
+        gcopy(8, z, other(blk_d(z)), sib).wait_recv()
+        return carry
+
+    lax.fori_loop(0, per_group, onward, 0)
+    lax.fori_loop(per_group, depth, spread_z, 0)
+    lax.fori_loop(0, per_group, last, 0)
+    lax.fori_loop(per_group, depth, onward, 0)
 
     images = devices // group
     quads = HEADS // pieces
 
-    def lay(it, carry):
-        image, quad = it // quads, lax.rem(it, quads)
+    def lay(image, quad):
         first = image * group + quad * pieces
         cols = []
         for g in range(pieces):
@@ -268,29 +282,19 @@
             pl.ds(pl.multiple_of(image * n_q, n_q), n_q),
             pl.ds(pl.multiple_of(quad * span, LANES), span),
         ] = jnp.concatenate(cols, axis=1)
-        return carry
-
-    lax.fori_loop(0, images * quads, lay, 0)
-
-    own_rows[...] = proj[pl.ds(pl.multiple_of(me * rows_dev, rows_dev), rows_dev), :]
     expert = me // 2
-    lane_row = lax.broadcasted_iota(jnp.int32, (rows_dev, LANES), 1)
+    lane_row = lax.rem(lane, split)
 
     def norm_rows(d, carry):
         rows = pl.ds(pl.multiple_of(d * rows_dev, rows_dev), rows_dev)
         x = proj[rows, :].astype(F32)
         r = lax.rsqrt(jnp.mean(x * x, axis=1, keepdims=True) + 1e-06)
-        proj[rows, :] = (x * r * gain_ref[...]).astype(BF16)
-        share = gath[d, main + part : main + part + rows_dev, :].astype(F32) + gath[
-            d, main + part + rows_dev : main + part + 2 * rows_dev, :
-        ].astype(F32)
+        proj[rows, :] = (x * r * gain_ref[...].reshape(1, -1)).astype(BF16)
+        share = gath[d, main + part : main + part + rows_dev, :].astype(F32)
         mine = jnp.sum(jnp.where(lane_row == expert, share, 0.0), axis=1, keepdims=True)
         gates[rows, :] = jnp.broadcast_to(mine, (rows_dev, LANES))
         return carry
 
-    lax.fori_loop(0, devices, norm_rows, 0)
-    for c in w_copies:
-        c.wait()
 
     block_rows = n_q
     z_block = block_rows // (8 * rows_dev)
@@ -302,7 +306,7 @@
             src.at[1 - core, :, z], dst.at[:, z], s1_send.at[side, z], s1_recv.at[side, z], sib
         )
 
-    def experts(r, carry):
+    def experts(r):
         rows = pl.ds(pl.multiple_of(r * block_rows, block_rows), block_rows)
         x = proj[rows, :]
         dims = (((1,), (1,)), ((), ()))
@@ -327,9 +331,6 @@
         for z in range(z_block):
             s1(r * z_block + z, 0).start()
             s1(r * z_block + z, 1).start()
-        return carry
-
-    lax.fori_loop(0, devices * rows_dev // block_rows, experts, 0)
 
     def add_into(dst, d_ix, others):
         total = dst[d_ix].astype(F32)
@@ -343,7 +344,8 @@
     def s2b(z):
         return rcopy(pb.at[core, 1 - yi, z], r2b.at[z], s2_send.at[1, z], s2_recv.at[1, z], yn)
 
-    def home1(z, carry):
+    def home1(i, carry):
+        z = zo(i)
         s1(z, 0).wait_recv()
         pa[core, 1 - xi, z] = add_into(pa, (core, 1 - xi, z), [(r1a, (1 - xi, z))])
         s2a(z).start()
@@ -352,8 +354,6 @@
         s2b(z).start()
         return carry
 
-    lax.fori_loop(0, depth, home1, 0)
-
     def s3a(z):
         return rcopy(
             pa.at[core, xi, z, 1 - yi], r3a.at[z], s3_send.at[0, z], s3_recv.at[0, z], yn
@@ -364,7 +364,8 @@
             pb.at[core, yi, z, 1 - xi], r3b.at[z], s3_send.at[1, z], s3_recv.at[1, z], xn
         )
 
-    def home2(z, carry):
+    def home2(i, carry):
+        z = zo(i)
         s2a(z).wait_recv()
         pa[core, xi, z] = add_into(pa, (core, xi, z), [(r1a, (xi, z)), (r2a, z)])
         s3a(z).start()
@@ -373,44 +374,83 @@
         s3b(z).start()
         return carry
 
-    lax.fori_loop(0, depth, home2, 0)
-
-    def s4(dz, side):
-        zt = lax.rem(zi + dz, depth)
+    def s4(zt, side):
         src = ua if side == 0 else ub
         dst = r4a if side == 0 else r4b
         return rcopy(
-            src.at[zt], dst.at[dz], s4_send.at[side, dz], s4_recv.at[side, dz],
-            dev(zt, yi, xi, core),
-        )
-
-    def home3(dz, carry):
-        z = lax.rem(zi + dz, depth)
+            src.at[zt], dst.at[zi], s4_send.at[side, zt], s4_recv.at[side, zi], own(zt)
+        )
+
+    def s4_in(z, side):
+        dst = r4a if side == 0 else r4b
+        return rcopy(
+            dst.at[z], dst.at[z], s4_send.at[side, z], s4_recv.at[side, z], own(z)
+        )
+
+    def home3(i, carry):
+        z = zo(i)
         s3a(z).wait_recv()
         ua[z] = add_into(pa, (core, xi, z, yi), [(r3a, z)])
         s3b(z).wait_recv()
         ub[z] = add_into(pb, (core, yi, z, xi), [(r3b, z)])
 
-        @pl.when(dz > 0)
+        @pl.when(i > 0)
         def _():
-            s4(dz, 0).start()
-            s4(dz, 1).start()
-
-        return carry
-
-    def far_first(i, carry):
-        return home3(depth - 1 - i, carry)
-
-    lax.fori_loop(0, depth, far_first, 0)
+            s4(z, 0).start()
+            s4(z, 1).start()
+
+        return carry
+
+    def each(i, carry):
+        image = lax.rem(zi // per_group + i, images)
+        first, end = per_group * i, per_group * (i + 1)
+
+        @pl.when(i > 0)
+        def _():
+            lax.fori_loop(first, end, last, 0)
+            lax.fori_loop(first - per_group, first, home1, 0)
+
+        lax.fori_loop(first, end, from_sib, 0)
+
+        def lay_quad(quad, c):
+            lay(image, quad)
+            return c
+
+        lax.fori_loop(0, quads, lay_quad, 0)
+
+        @pl.when(i == 0)
+        def _():
+            own_rows[...] = proj[pl.ds(pl.multiple_of(me * rows_dev, rows_dev), rows_dev), :]
+            for c in w_copies:
+                c.wait()
+
+        lax.fori_loop(image * group, image * group + group, norm_rows, 0)
+
+        @pl.when(i > 0)
+        def _():
+            lax.fori_loop(first - per_group, first, home2, 0)
+
+        experts(image)
+
+        @pl.when(i > 0)
+        def _():
+            lax.fori_loop(first - per_group, first, home3, 0)
+
+        return carry
+
+    lax.fori_loop(0, images, each, 0)
+    for home in (home1, home2, home3):
+        lax.fori_loop(depth - per_group, depth, home, 0)
     mine = own_rows[...].astype(F32)
     sum_a = mine[:, :half_w] + ua[zi].astype(F32)
     sum_b = mine[:, half_w:] + ub[zi].astype(F32)
 
-    def home4(dz, carry):
+    def home4(i, carry):
         left, right = carry
-        s4(dz, 0).wait_recv()
-        s4(dz, 1).wait_recv()
-        return left + r4a[dz].astype(F32), right + r4b[dz].astype(F32)
+        z = zo(i)
+        s4_in(z, 0).wait_recv()
+        s4_in(z, 1).wait_recv()
+        return left + r4a[z].astype(F32), right + r4b[z].astype(F32)
 
     sum_a, sum_b = lax.fori_loop(1, depth, home4, (sum_a, sum_b))
     out_ref[:, :half_w] = sum_a.astype(BF16)
@@ -422,10 +462,10 @@
 
     lax.fori_loop(1, group, sent_kv, 0)
 
-    def sent_z(dz, carry):
-        z_out(dz).wait_send()
-        s4(dz, 0).wait_send()
-        s4(dz, 1).wait_send()
+    def sent_z(i, carry):
+        z_out(i).wait_send()
+        s4(zo(i), 0).wait_send()
+        s4(zo(i), 1).wait_send()
         return carry
 
     lax.fori_loop(1, depth, sent_z, 0)
@@ -454,6 +494,7 @@
     patches, vision = patch_keys.shape
     width = patch_values.shape[1]
     rows_dev = route_experts.shape[0]
+    assert devices // 2 <= LANES // 2
     hidden = w_gate.shape[0]
     depth = devices // 8
     group = HEADS
@@ -462,12 +503,15 @@
     extra = value_size - LANES
     pieces = LANES // extra
     wide_kv = -(-(value_size + vision // HEADS) // LANES) * LANES
-    tall = n_q + n_q // pieces + 2 * rows_dev
+    tall = n_q + n_q // pieces + rows_dev
     rows = devices * rows_dev
     half = width // 2
     vm = pltpu.VMEM
     dma = pltpu.SemaphoreType.DMA
     scratch = [
+        vm(queries.shape, BF16),
+        vm(patch_keys.shape, BF16),
+        vm(patch_values.shape, BF16),
         vm((group, patches, wide_kv), BF16),
         vm((group, patches, wide_kv), BF16),
         vm((n_q, group * patches), F32),
@@ -492,7 +536,7 @@
         vm((depth, rows_dev, half), BF16),
         vm((depth, rows_dev, half), BF16),
         vm((depth, rows_dev, half), BF16),
-        dma((3,)),
+        dma((6,)),
         dma((group,)), dma((group,)),
         dma((9, depth)), dma((9, depth)),
         dma((2, depth)), dma((2, depth)),
@@ -505,14 +549,14 @@
     return pl.pallas_call(
         functools.partial(kernel, devices),
         out_shape=jax.ShapeDtypeStruct((rows_dev, width), BF16),
-        in_specs=[vspec] * 6 + [hspec] * 3,
+        in_specs=[hspec] * 3 + [vspec] * 3 + [hspec] * 3,
         out_specs=vspec,
         scratch_shapes=scratch,
         compiler_params=pltpu.CompilerParams(
             collective_id=0, has_side_effects=True, vmem_limit_bytes=62 * 1024 * 1024
         ),
     )(
-        queries, patch_keys, patch_values, norm_gain.reshape(1, -1), route_experts, route_weights,
+        queries, patch_keys, patch_values, norm_gain, route_experts.T, route_weights.T,
         w_gate, w_up, w_down,
     )
 

time: 86 us -> 74.9 us (0.87)
  Pallas kernels: 80.1 us -> 73.1 us
  local copies, waits for them, and re-layouts: 5.56 us -> 1.53 us
    pallas_call x1, Pallas kernels: 80.1 us -> 73.1 us  [on_device(): pl.pallas_call(functools.partial(kernel, devices), out_shape=jax.ShapeDty...]
    unnamed x3 -> x1, local copies, waits for them, and re-layouts: 4.24 us -> 1.53 us
    reshape x1 -> x0, local copies, waits for them, and re-layouts: 1.31 us -> none  [on_device(): norm_gain.reshape(1, -1)]
where the time goes in v2:
time: 74.9 us; the launch traced here: 74.7 us
  Pallas kernels  73.1 us (98%)
  local copies, waits for them, and re-layouts  1.53 us (2%)
    pallas_call x1, Pallas kernels, on_device(): pl.pallas_call(functools.partial(kernel, devices), out_shape=jax.ShapeDty...  73.1 us
    unnamed x1, local copies, waits for them, and re-layouts  1.53 us

profile of v2, /device:TPU:0, one launch (start us, length us, event | category | flops | bytes accessed | tf_op | source)
XLA Modules:
  0.0 74.7 jit_solution(12043439088154126083)
XLA Ops:
  0.0 73.1 %shard_map.91 = bf16[16,2560]{1,0:T(8,128)(2,1)} custom-call(bf16[256,1152]{1,0:T(8,128)(2,1)} %q_hbm.1, bf16[128,1152]{1,0:T(8,128)(2,1)} %k_hbm.1, bf16[128,2560]{1,0:T(8,128)(2,1)} %v_hbm.1, f32[2560]{0:T(1024)} %gain_ref.1, s32[6,16]{1,0:T(8,128)} %bitcast.2, s32[6,16]{1,0:T(8,128)} %bitcast.3, bf16[512,2560]{1,0:T(8,128)(2,1)} %wg_hbm.1, ...), custom_call_target="tpu_custom_call" | custom-call | tf_op jit(solution)/shard_map/pallas_call | solution.py:549
  73.1 1.5 %copy.11 = bf16[16,2560]{1,0:T(8,128)(2,1)} copy(bf16[16,2560]{1,0:T(8,128)(2,1)} %shard_map.91) | data formatting | bytes 163840

commit v3 on v2

--- a/solution.py
+++ b/solution.py
@@ -141,17 +141,14 @@
     table_hi = table.astype(BF16).astype(F32)
     table = jnp.where(lane < split, table_hi, table - table_hi).astype(BF16)
 
-    def wait_kv(k, carry):
-        a2a_in(k).wait_recv()
-        return carry
-
-    lax.fori_loop(1, group, wait_kv, 0)
-
     scale = key_size ** (-0.5)
-    for s in range(group):
-        s_scr[:, s * patches : (s + 1) * patches] = (
+    for k in range(group):
+        if k > 0:
+            a2a_in(k).wait_recv()
+        s_scr[:, k * patches : (k + 1) * patches] = (
             lax.dot_general(
-                q_pad, kvr[s], (((1,), (1,)), ((), ())), preferred_element_type=F32
+                q_pad, kvr[lax.rem(spot + group - k, group)], (((1,), (1,)), ((), ())),
+                preferred_element_type=F32,
             )
             * scale
         )
@@ -170,7 +167,9 @@
     acc = jnp.zeros((n_q, wide_kv), F32)
     for s in range(group):
         acc = acc + jnp.dot(
-            p_scr[:, s * patches : (s + 1) * patches], kvr[s], preferred_element_type=F32
+            p_scr[:, s * patches : (s + 1) * patches],
+            kvr[lax.rem(spot + group - s, group)],
+            preferred_element_type=F32,
         )
     att = (acc / tot_scr[:, 0:1]).astype(BF16)
     main = n_q

time: 74.9 us -> 73.5 us (0.981)
  Pallas kernels: 73.1 us -> 71.7 us
    pallas_call x1, Pallas kernels: 73.1 us -> 71.7 us  [on_device(): pl.pallas_call(functools.partial(kernel, devices), out_shape=jax.ShapeDty...]
where the time goes in v3:
time: 73.5 us; the launch traced here: 73.3 us
  Pallas kernels  71.7 us (98%)
  local copies, waits for them, and re-layouts  1.53 us (2%)
    pallas_call x1, Pallas kernels, on_device(): pl.pallas_call(functools.partial(kernel, devices), out_shape=jax.ShapeDty...  71.7 us
    unnamed x1, local copies, waits for them, and re-layouts  1.53 us

profile of v3, /device:TPU:0, one launch (start us, length us, event | category | flops | bytes accessed | tf_op | source)
XLA Modules:
  0.0 73.3 jit_solution(9942935441891321713)
XLA Ops:
  0.0 71.7 %shard_map.91 = bf16[16,2560]{1,0:T(8,128)(2,1)} custom-call(bf16[256,1152]{1,0:T(8,128)(2,1)} %q_hbm.1, bf16[128,1152]{1,0:T(8,128)(2,1)} %k_hbm.1, bf16[128,2560]{1,0:T(8,128)(2,1)} %v_hbm.1, f32[2560]{0:T(1024)} %gain_ref.1, s32[6,16]{1,0:T(8,128)} %bitcast.2, s32[6,16]{1,0:T(8,128)} %bitcast.3, bf16[512,2560]{1,0:T(8,128)(2,1)} %wg_hbm.1, ...), custom_call_target="tpu_custom_call" | custom-call | tf_op jit(solution)/shard_map/pallas_call | solution.py:548
  71.7 1.5 %copy.11 = bf16[16,2560]{1,0:T(8,128)(2,1)} copy(bf16[16,2560]{1,0:T(8,128)(2,1)} %shard_map.91) | data formatting | bytes 163840
